TPU v7x, 32 devices: a whole 2x2x4 slice. The times are simulated.
32 devices in a mesh: fsdp: 16 (over z, y, core), tensor: 2 (over x).
Axes of the slice: x: 2, y: 2, z: 4, core: 2. Of those that a mesh axis runs over, the one named last changes fastest.
Arguments:
- images: float32 [16, 200, 384], P('fsdp', 'tensor'), may hold values from -6 to 6
- upstream: float32 [16, 200, 384], P('fsdp', 'tensor'), may hold values from -6 to 6
- image_count: int32 [16], P('fsdp'), may hold values from 0 to 1, as said below
- valid_tokens: int32 [16], P('fsdp'), may hold values from 165 to 197, as said below
- qkv_weight: bfloat16 [2, 3, 384, 384], P(None, None, 'fsdp', 'tensor'), may hold values from -0.3125 to 0.3125
- qv_bias: float32 [2, 2, 384], replicated, may hold values from -2 to 2
- out_weight: bfloat16 [2, 384, 384], P(None, 'tensor', 'fsdp'), may hold values from -1.25 to 1.25
- out_bias: float32 [2, 384], replicated, may hold values from -2 to 2
- gain_one: float32 [2, 384], replicated, may hold values from 0.1 to 1.9
- shift_one: float32 [2, 384], replicated, may hold values from -2 to 2
- gain_two: float32 [2, 384], replicated, may hold values from 0.1 to 1.9
- shift_two: float32 [2, 384], replicated, may hold values from -2 to 2
- up_weight: bfloat16 [2, 384, 1536], P(None, 'fsdp', 'tensor'), may hold values from -0.3125 to 0.3125
- up_bias: float32 [2, 1536], replicated, may hold values from -2 to 2
- down_weight: bfloat16 [2, 1536, 384], P(None, 'tensor', 'fsdp'), may hold values from -0.15625 to 0.15625
- down_bias: float32 [2, 384], replicated, may hold values from -2 to 2
Outputs:
- output: float32 [16, 200, 384], P('fsdp', 'tensor')
- grad_images: float32 [16, 200, 384], P('fsdp', 'tensor')
- qkv_grad: float32 [2, 3, 384, 384], P(None, None, 'fsdp', 'tensor')
- qv_bias_grad: float32 [2, 2, 384], replicated
- out_grad: float32 [2, 384, 384], P(None, 'tensor', 'fsdp')
- out_bias_grad: float32 [2, 384], replicated
- gain_one_grad: float32 [2, 384], replicated
- shift_one_grad: float32 [2, 384], replicated
- gain_two_grad: float32 [2, 384], replicated
- shift_two_grad: float32 [2, 384], replicated
- up_grad: float32 [2, 384, 1536], P(None, 'fsdp', 'tensor')
- up_bias_grad: float32 [2, 1536], replicated
- down_grad: float32 [2, 1536, 384], P(None, 'tensor', 'fsdp')
- down_bias_grad: float32 [2, 384], replicated
Inputs may be any that keep to these rules, and one draw needn't show every extreme that they name: `image_count`: the live images of an index of fsdp fill its first slots; some index holds 1. `valid_tokens`: some slot has 197 tokens that count.
All inputs are finite; a program needn't handle non-finite values.
Results may differ from a plain program's by a relative error of at most 0.02.
Values may be sent and summed in bfloat16 or wider, within the bound.
A program may use at most 128 MiB of HBM per device.

v0:
```python
from functools import partial

import jax
import jax.numpy as jnp
from jax import lax
from jax.sharding import PartitionSpec as P

D = 384
HD = 64
FF = 1536


epsilon = 1e-06


def norm_rows(hidden, gain, shift):
    centre = hidden - jnp.mean(hidden, axis=-1, keepdims=True)
    spread = jnp.mean(centre * centre, axis=-1, keepdims=True)
    return centre * lax.rsqrt(spread + epsilon) * gain + shift


def take_half(vector, width_here, index):
    return lax.dynamic_slice_in_dim(vector, index * width_here, width_here, vector.ndim - 1)


def widen_half(vector, index, total):
    empty = jnp.zeros(vector.shape[:-1] + (total,), jnp.float32)
    return lax.dynamic_update_slice_in_dim(empty, vector, index * vector.shape[-1], vector.ndim - 1)


def head_split(array):
    slot_count, length, head_width = array.shape
    return array.reshape(slot_count, length, head_width // HD, HD)


def masked_scores(queries, key_rows, key_ok):
    scores = jnp.einsum(
        "sqhd,skhd->shqk",
        head_split(queries),
        head_split(key_rows),
        preferred_element_type=jnp.float32,
    ) * HD ** (-0.5)
    return jnp.where(key_ok[:, None, None, :], scores, -1e30)


def attend(queries, key_rows, values, key_ok):
    scores = masked_scores(queries, key_rows, key_ok)
    highest_score = jnp.max(scores, axis=-1, keepdims=True)
    log_total = highest_score + jnp.log(
        jnp.sum(jnp.exp(scores - highest_score), axis=-1, keepdims=True)
    )
    portions = jnp.exp(scores - log_total).astype(jnp.bfloat16)
    mixed = jnp.einsum(
        "shqk,skhd->sqhd", portions, head_split(values), preferred_element_type=jnp.float32
    )
    return (log_total, mixed.reshape(queries.shape).astype(jnp.bfloat16))


def attend_back(queries, key_rows, values, log_total, grad_mixed, key_ok):
    portions = jnp.exp(masked_scores(queries, key_rows, key_ok) - log_total)
    grad_heads = head_split(grad_mixed)
    grad_portions = jnp.einsum(
        "sqhd,skhd->shqk", grad_heads, head_split(values), preferred_element_type=jnp.float32
    )
    grad_values = jnp.einsum(
        "shqk,sqhd->skhd",
        portions.astype(jnp.bfloat16),
        grad_heads,
        preferred_element_type=jnp.float32,
    )
    inner_sum = jnp.sum(portions * grad_portions, axis=-1, keepdims=True)
    grad_scores = (portions * (grad_portions - inner_sum)).astype(jnp.bfloat16)
    grad_queries = jnp.einsum(
        "shqk,skhd->sqhd", grad_scores, head_split(key_rows), preferred_element_type=jnp.float32
    ) * HD ** (-0.5)
    grad_keys = jnp.einsum(
        "shqk,sqhd->skhd", grad_scores, head_split(queries), preferred_element_type=jnp.float32
    ) * HD ** (-0.5)
    full_shape = queries.shape
    return (
        grad_queries.reshape(full_shape).astype(jnp.bfloat16),
        grad_keys.reshape(full_shape).astype(jnp.bfloat16),
        grad_values.reshape(full_shape).astype(jnp.bfloat16),
    )


def fetch_weights(qkv_part, out_part, up_part, down_part):
    return (
        lax.all_gather(qkv_part, "fsdp", axis=1, tiled=True),
        lax.all_gather(out_part, "fsdp", axis=1, tiled=True),
        lax.all_gather(up_part, "fsdp", axis=0, tiled=True),
        lax.all_gather(down_part, "fsdp", axis=1, tiled=True),
    )


def share_tokens(value):
    return lax.all_gather(value, "tensor", axis=1, tiled=True)


def sum_branch(value):
    return lax.psum_scatter(
        value.astype(jnp.bfloat16), "tensor", scatter_dimension=1, tiled=True
    ).astype(jnp.float32)


def gather_grads(value):
    return lax.all_gather(value, "tensor", axis=1, tiled=True)


def sum_inputs(value):
    return lax.psum_scatter(
        value.astype(jnp.bfloat16), "tensor", scatter_dimension=1, tiled=True
    ).astype(jnp.float32)


def local(
    images,
    upstream,
    image_count,
    valid_tokens,
    qkv_weight,
    qv_bias,
    out_weight,
    out_bias,
    gain_one,
    shift_one,
    gain_two,
    shift_two,
    up_weight,
    up_bias,
    down_weight,
    down_bias,
):
    slot_count, half_length, model_width = images.shape
    tensor_size = lax.axis_size("tensor")
    tensor_rank = lax.axis_index("tensor")
    length = half_length * tensor_size
    head_width = qkv_weight.shape[3]
    hidden_width = up_weight.shape[2]
    layer_count = qkv_weight.shape[0]
    key_ok = jnp.arange(length, dtype=jnp.int32)[None, :] < valid_tokens[:, None]
    slot_live = jnp.arange(slot_count, dtype=jnp.int32) < image_count[0]
    own_rows = tensor_rank * half_length + jnp.arange(half_length, dtype=jnp.int32)
    row_ok = jnp.where(
        (own_rows[None, :] < valid_tokens[:, None]) & slot_live[:, None], 1.0, 0.0
    ).astype(jnp.float32)
    stored = []
    hidden = images
    for layer_index in range(layer_count):
        fetched = fetch_weights(
            qkv_weight[layer_index],
            out_weight[layer_index],
            up_weight[layer_index],
            down_weight[layer_index],
        )
        qkv_full, out_full, up_full, down_full = fetched
        bias_pair = take_half(qv_bias[layer_index], head_width, tensor_rank)
        normed = norm_rows(hidden, gain_one[layer_index], shift_one[layer_index]).astype(
            jnp.bfloat16
        )
        shared = share_tokens(normed)
        project = jnp.einsum("std,cde->cste", shared, qkv_full, preferred_element_type=jnp.float32)
        queries = (project[0] + bias_pair[0]).astype(jnp.bfloat16)
        key_rows = project[1].astype(jnp.bfloat16)
        values = (project[2] + bias_pair[1]).astype(jnp.bfloat16)
        log_total, mixed = attend(queries, key_rows, values, key_ok)
        branch = sum_branch(
            jnp.einsum("ste,ed->std", mixed, out_full, preferred_element_type=jnp.float32)
        )
        middle = hidden + (branch + out_bias[layer_index])
        normed_two = norm_rows(middle, gain_two[layer_index], shift_two[layer_index]).astype(
            jnp.bfloat16
        )
        shared_two = share_tokens(normed_two)
        up_value = jnp.einsum(
            "std,df->stf", shared_two, up_full, preferred_element_type=jnp.float32
        ) + take_half(up_bias[layer_index], hidden_width, tensor_rank)
        activated = jax.nn.gelu(up_value, approximate=False).astype(jnp.bfloat16)
        branch_two = sum_branch(
            jnp.einsum("stf,fd->std", activated, down_full, preferred_element_type=jnp.float32)
        )
        stored.append(
            (
                hidden,
                shared,
                queries,
                key_rows,
                values,
                log_total,
                mixed,
                middle,
                shared_two,
                up_value,
                activated,
                fetched,
            )
        )
        hidden = middle + (branch_two + down_bias[layer_index])
    output = hidden * row_ok[:, :, None]
    grad_hidden = upstream * row_ok[:, :, None]
    large_grads = [None] * layer_count
    small_grads = [None] * layer_count
    for layer_index in reversed(range(layer_count)):
        (
            hidden_in,
            shared,
            queries,
            key_rows,
            values,
            log_total,
            mixed,
            middle,
            shared_two,
            up_value,
            activated,
            fetched,
        ) = stored[layer_index]
        qkv_full, out_full, up_full, down_full = (
            lax.all_gather(qkv_weight[layer_index], "fsdp", axis=1, tiled=True),
            lax.all_gather(out_weight[layer_index], "fsdp", axis=1, tiled=True),
            lax.all_gather(up_weight[layer_index], "fsdp", axis=0, tiled=True),
            lax.all_gather(down_weight[layer_index], "fsdp", axis=1, tiled=True),
        )
        grad_branch = grad_hidden.astype(jnp.bfloat16)
        down_bias_grad = jnp.sum(grad_branch.astype(jnp.float32), axis=(0, 1))
        grad_rows = gather_grads(grad_branch)
        down_grad = jnp.einsum(
            "stf,std->fd", activated, grad_rows, preferred_element_type=jnp.float32
        )
        grad_activated = jnp.einsum(
            "std,fd->stf", grad_rows, down_full, preferred_element_type=jnp.float32
        )
        gelu_back = jax.vjp(partial(jax.nn.gelu, approximate=False), up_value)[1]
        grad_up = gelu_back(grad_activated)[0].astype(jnp.bfloat16)
        up_bias_grad = widen_half(
            jnp.sum(grad_up.astype(jnp.float32), axis=(0, 1)), tensor_rank, FF
        )
        up_grad = jnp.einsum("std,stf->df", shared_two, grad_up, preferred_element_type=jnp.float32)
        grad_normed_two = sum_inputs(
            jnp.einsum("stf,df->std", grad_up, up_full, preferred_element_type=jnp.float32)
        )
        norm_back = jax.vjp(norm_rows, middle, gain_two[layer_index], shift_two[layer_index])[1]
        grad_from_norm, gain_two_grad, shift_two_grad = norm_back(grad_normed_two)
        grad_middle = grad_hidden + grad_from_norm
        grad_branch = grad_middle.astype(jnp.bfloat16)
        out_bias_grad = jnp.sum(grad_branch.astype(jnp.float32), axis=(0, 1))
        grad_rows = gather_grads(grad_branch)
        out_grad = jnp.einsum("ste,std->ed", mixed, grad_rows, preferred_element_type=jnp.float32)
        grad_mixed = jnp.einsum(
            "std,ed->ste", grad_rows, out_full, preferred_element_type=jnp.float32
        ).astype(jnp.bfloat16)
        grad_queries, grad_keys, grad_values = attend_back(
            queries, key_rows, values, log_total, grad_mixed, key_ok
        )
        grad_project = jnp.stack([grad_queries, grad_keys, grad_values])
        qkv_grad = jnp.einsum(
            "std,cste->cde", shared, grad_project, preferred_element_type=jnp.float32
        )
        qv_sums = jnp.stack(
            [
                jnp.sum(grad_queries.astype(jnp.float32), axis=(0, 1)),
                jnp.sum(grad_values.astype(jnp.float32), axis=(0, 1)),
            ]
        )
        qv_bias_grad = widen_half(qv_sums, tensor_rank, D)
        grad_normed = sum_inputs(
            jnp.einsum("cste,cde->std", grad_project, qkv_full, preferred_element_type=jnp.float32)
        )
        norm_back = jax.vjp(norm_rows, hidden_in, gain_one[layer_index], shift_one[layer_index])[1]
        grad_input, gain_one_grad, shift_one_grad = norm_back(grad_normed)
        grad_hidden = grad_middle + grad_input
        large_grads[layer_index] = (
            lax.psum_scatter(qkv_grad, "fsdp", scatter_dimension=1, tiled=True),
            lax.psum_scatter(out_grad, "fsdp", scatter_dimension=1, tiled=True),
            lax.psum_scatter(up_grad, "fsdp", scatter_dimension=0, tiled=True),
            lax.psum_scatter(down_grad, "fsdp", scatter_dimension=1, tiled=True),
        )
        small_grads[layer_index] = (
            qv_bias_grad,
            out_bias_grad,
            gain_one_grad,
            shift_one_grad,
            gain_two_grad,
            shift_two_grad,
            up_bias_grad,
            down_bias_grad,
        )
    stacked = tuple(
        (
            jnp.stack([large_grads[layer_index][member] for layer_index in range(layer_count)])
            for member in range(4)
        )
    )
    small_stacked = tuple(
        (
            jnp.stack([small_grads[layer_index][member] for layer_index in range(layer_count)])
            for member in range(8)
        )
    )
    summed = lax.psum(
        (
            small_stacked[0],
            small_stacked[1],
            small_stacked[2],
            small_stacked[3],
            small_stacked[4],
            small_stacked[5],
            small_stacked[6],
            small_stacked[7],
        ),
        ("fsdp", "tensor"),
    )
    return (
        output,
        grad_hidden,
        stacked[0],
        summed[0],
        stacked[1],
        summed[1],
        summed[2],
        summed[3],
        summed[4],
        summed[5],
        stacked[2],
        summed[6],
        stacked[3],
        summed[7],
    )


def solution(mesh):
    in_specs = (
        P("fsdp", "tensor", None),
        P("fsdp", "tensor", None),
        P("fsdp"),
        P("fsdp"),
        P(None, None, "fsdp", "tensor"),
        P(),
        P(None, "tensor", "fsdp"),
        P(),
        P(),
        P(),
        P(),
        P(),
        P(None, "fsdp", "tensor"),
        P(),
        P(None, "tensor", "fsdp"),
        P(),
    )
    out_specs = (
        P("fsdp", "tensor", None),
        P("fsdp", "tensor", None),
        P(None, None, "fsdp", "tensor"),
        P(),
        P(None, "tensor", "fsdp"),
        P(),
        P(),
        P(),
        P(),
        P(),
        P(None, "fsdp", "tensor"),
        P(),
        P(None, "tensor", "fsdp"),
        P(),
    )
    return jax.shard_map(local, mesh=mesh, in_specs=in_specs, out_specs=out_specs, check_vma=False)
```

profile of v0, /device:TPU:0, one launch (start us, length us, event | category | flops | bytes accessed | tf_op | source)
XLA Modules:
  0.0 821.0 jit_solution(5167804713324282642)
XLA Ops:
  7.2 1.7 reduce_sum.331
  9.0 2.4 multiply_reduce_fusion.13
  13.5 7.6 all_gather.56
  21.1 23.7 %all-gather = bf16[1,3,384,192]{3,2,1,0:T(8,128)(2,1)S(1)} all-gather(bf16[1,3,24,192]{3,2,1,0:T(8,128)(2,1)S(1)} %get-tuple-element.113), channel_id=2, replica_groups=mesh['fsdp'=16,'tensor'=2] {'fsdp'}, dimensions={2}, use_global_device_ids=true | all-gather | bytes 470016 | tf_op jit(solution)/shard_map/all_gather | solution.py:89
  48.0 18.0 %all-gather.1 = bf16[1,192,384]{1,2,0:T(8,128)(2,1)S(1)} all-gather(bf16[1,192,24]{1,2,0:T(8,128)(2,1)S(1)} %get-tuple-element.115), channel_id=3, replica_groups=mesh['fsdp'=16,'tensor'=2] {'fsdp'}, dimensions={2}, use_global_device_ids=true | all-gather | bytes 156672 | tf_op jit(solution)/shard_map/all_gather | solution.py:90
  66.5 7.6 fusion
  74.2 2.4 collective-permute-start
  77.9 20.4 %all-gather.2 = bf16[1,384,768]{2,1,0:T(8,128)(2,1)S(1)} all-gather(bf16[1,24,768]{2,1,0:T(8,128)(2,1)S(1)} %get-tuple-element.111), channel_id=4, replica_groups=mesh['fsdp'=16,'tensor'=2] {'fsdp'}, dimensions={1}, use_global_device_ids=true | all-gather | bytes 626688 | tf_op jit(solution)/shard_map/all_gather | solution.py:91
  98.3 20.6 %all-gather.3 = bf16[1,768,384]{1,2,0:T(8,128)(2,1)} all-gather(bf16[1,768,24]{1,2,0:T(8,128)(2,1)S(1)} %get-tuple-element.109), channel_id=5, replica_groups=mesh['fsdp'=16,'tensor'=2] {'fsdp'}, dimensions={2}, use_global_device_ids=true | all-gather | bytes 626688 | tf_op jit(solution)/shard_map/all_gather | solution.py:92
  118.9 22.1 %all-gather.4 = bf16[1,3,384,192]{3,2,1,0:T(8,128)(2,1)} all-gather(bf16[1,3,24,192]{3,2,1,0:T(8,128)(2,1)S(1)} %get-tuple-element.112), channel_id=6, replica_groups=mesh['fsdp'=16,'tensor'=2] {'fsdp'}, dimensions={2}, use_global_device_ids=true | all-gather | bytes 470016 | tf_op jit(solution)/shard_map/all_gather | solution.py:89
  140.9 20.4 %all-gather.6 = bf16[1,384,768]{2,1,0:T(8,128)(2,1)} all-gather(bf16[1,24,768]{2,1,0:T(8,128)(2,1)S(1)} %get-tuple-element.110), channel_id=8, replica_groups=mesh['fsdp'=16,'tensor'=2] {'fsdp'}, dimensions={1}, use_global_device_ids=true | all-gather | bytes 626688 | tf_op jit(solution)/shard_map/all_gather | solution.py:91
  162.0 20.6 %all-gather.7 = bf16[1,768,384]{1,2,0:T(8,128)(2,1)S(1)} all-gather(bf16[1,768,24]{1,2,0:T(8,128)(2,1)S(1)} %get-tuple-element.108), channel_id=9, replica_groups=mesh['fsdp'=16,'tensor'=2] {'fsdp'}, dimensions={2}, use_global_device_ids=true | all-gather | bytes 626688 | tf_op jit(solution)/shard_map/all_gather | solution.py:92
  189.7 6.9 all_gather.59
  196.6 2.5 multiply_convert_fusion.3
  200.2 6.4 fusion.1
  207.3 4.2 collective-permute-start.1
  211.5 17.8 %all-gather.5 = bf16[1,192,384]{1,2,0:T(8,128)(2,1)S(1)} all-gather(bf16[1,192,24]{1,2,0:T(8,128)(2,1)S(1)} %get-tuple-element.114), channel_id=7, replica_groups=mesh['fsdp'=16,'tensor'=2] {'fsdp'}, dimensions={2}, use_global_device_ids=true | all-gather | bytes 156672 | tf_op jit(solution)/shard_map/all_gather | solution.py:90
  231.7 1.7 concatenate.1
  233.4 1.7 fusion.141
  237.6 7.1 all_gather.62
  247.3 6.4 fusion.2
  253.7 3.7 collective-permute-start.2
  257.3 6.2 all_gather.68
  264.6 1.7 fusion.139
  268.8 6.0 all_gather.65
  274.8 3.4 multiply_convert_fusion.2
  281.1 8.8 %fusion.4 = bf16[112,384]{1,0:T(8,128)(2,1)S(1)} fusion(bf16[1,200,384]{2,1,0:T(8,128)(2,1)} %fusion.16), kind=kCustom, calls=%all-reduce-scatter.4 | all-reduce-scatter fusion | flops 86017 | bytes 240128
  289.9 2.6 collective-permute-start.4
  293.4 2.7 concatenate.4
  300.1 1.8 convert_reduce_fusion.8
  302.0 6.2 all_gather.69
  312.3 8.2 fusion.5
  321.1 1.9 collective-permute-start.5
  324.5 2.1 concatenate.5
  331.1 6.3 all_gather.70
  339.6 8.2 fusion.6
  347.8 1.9 collective-permute-start.6
  349.7 2.0 fusion.66
  357.5 5.9 all_gather.71
  378.7 7.3 fusion.133
  386.0 2.0 collective-permute-start.7
  391.8 39.9 %all-reduce.18 = (f32[2,2,384]{2,1,0:T(2,128)}, f32[2,384]{1,0:T(2,128)}, f32[2,384]{1,0:T(2,128)}, f32[2,384]{1,0:T(2,128)}, f32[2,384]{1,0:T(2,128)}, /*index=...) all-reduce(f32[2,2,384]{2,1,0:T(2,128)S(1)} %pad_maximum_fusion.5, ...), channel_id=1, replica_groups=mesh['fsdp'=16,'tensor'=2] {'fsdp','tensor'}, use_global_device_ids=true, to_apply=%region_36.37 | all-reduce | flops 9216 | bytes 73728 | tf_op jit(solution)/shard_map/psum | solution.py:300
  435.0 28.6 %reduce-scatter.31.cloned.1.call-done = f32[192,24]{0,1:T(8,128)} async-done(((f32[192,384]{0,1:T(8,128)}), f32[192,24]{0,1:T(8,128)}) %reduce-scatter.31.cloned.1.call-update) | async-done | bytes 18448 | tf_op jit(solution)/shard_map/reduce_scatter | solution.py:274
  465.0 104.9 %all-reduce.23.cloned.1.call-done = (f32[3,384,192]{2,0,1:T(4,128)}, f32[3,384,192]{2,0,1:T(4,128)}) async-done(((f32[3,384,192]{2,0,1:T(4,128)}, f32[3,384,192]{2,0,1:T(4,128)}), (f32[3,384,192]{2,0,1:T(4,128)}, f32[3,384,192]{2,0,1:T(4,128)})) %all-reduce.23.cloned.1.call-update) | async-done | bytes 1769488
  572.5 58.2 %reduce-scatter.41.cloned.1.call-done = f32[768,24]{0,1:T(8,128)} async-done(((f32[768,384]{0,1:T(8,128)}), f32[768,24]{0,1:T(8,128)}) %reduce-scatter.41.cloned.1.call-update) | async-done | bytes 73744 | tf_op jit(solution)/shard_map/reduce_scatter | solution.py:276
  630.7 60.6 %reduce-scatter.39.cloned.1.call-done = f32[768,24]{0,1:T(8,128)} async-done(((f32[768,384]{0,1:T(8,128)}), f32[768,24]{0,1:T(8,128)}) %reduce-scatter.39.cloned.1.call-update) | async-done | bytes 73744 | tf_op jit(solution)/shard_map/reduce_scatter | solution.py:276
  692.9 59.0 %reduce-scatter.37.cloned.1.call-done = f32[24,768]{1,0:T(8,128)} async-done(((f32[384,768]{1,0:T(8,128)}), f32[24,768]{1,0:T(8,128)}) %reduce-scatter.37.cloned.1.call-update) | async-done | bytes 73744 | tf_op jit(solution)/shard_map/reduce_scatter | solution.py:275
  751.9 60.7 %reduce-scatter.35.cloned.1.call-done = f32[24,768]{1,0:T(8,128)} async-done(((f32[384,768]{1,0:T(8,128)}), f32[24,768]{1,0:T(8,128)}) %reduce-scatter.35.cloned.1.call-update) | async-done | bytes 73744 | tf_op jit(solution)/shard_map/reduce_scatter | solution.py:275
  (415 shorter events, 79.6 us)
Async XLA Ops:
  7.2 13.9 %copy-start.58 = (bf16[2,3,24,192]{3,2,1,0:T(8,128)(2,1)S(1)}, bf16[2,3,24,192]{3,2,1,0:T(8,128)(2,1)}, u32[]{:S(2)}) copy-start(bf16[2,3,24,192]{3,2,1,0:T(8,128)(2,1)} %param.20) | copy-start | bytes 165892
  7.2 427.9 %reduce-scatter.33.cloned.1.call-start = ((), (), s32[]{:S(2)}) async-start(), calls=%async_computation.7 | async-start | bytes 417792 | tf_op jit(solution)/shard_map/reduce_scatter | solution.py:274
  21.1 24.4 %copy-start.32 = (bf16[1,200,384]{2,0,1:T(2,128)(2,1)}, bf16[1,200,384]{2,0,1:T(2,128)(2,1)S(1)}, u32[]{:S(2)}) copy-start(bf16[1,200,384]{2,0,1:T(2,128)(2,1)S(1)} %all_gather.56) | copy-start | bytes 460804
  45.6 20.7 %copy-start.7 = (f32[1,1,200,192]{2,3,0,1:T(8,128)}, f32[1,1,200,192]{2,3,0,1:T(8,128)S(1)}, u32[]{:S(2)}) copy-start(f32[1,1,200,192]{2,3,0,1:T(8,128)S(1)} %get-tuple-element.106) | copy-start | bytes 460804
  45.6 20.7 %copy-start.11 = (f32[1,1,200,192]{2,3,0,1:T(8,128)}, f32[1,1,200,192]{2,3,0,1:T(8,128)S(1)}, u32[]{:S(2)}) copy-start(f32[1,1,200,192]{2,3,0,1:T(8,128)S(1)} %get-tuple-element.107) | copy-start | bytes 460804
  45.6 20.6 %copy-start.39 = (bf16[1,1,200,192]{2,3,0,1:T(8,128)(2,1)}, bf16[1,1,200,192]{2,3,0,1:T(8,128)(2,1)S(1)}, u32[]{:S(2)}) copy-start(bf16[1,1,200,192]{2,3,0,1:T(8,128)(2,1)S(1)} %slice.183) | copy-start | bytes 230404
  46.6 19.7 %copy-start.62 = (f32[3,64]{1,0:T(4,128)}, f32[3,64]{1,0:T(4,128)S(1)}, u32[]{:S(2)}) copy-start(f32[3,64]{1,0:T(4,128)S(1)} %add.329) | copy-start | bytes 2308
  47.8 28.8 %copy-start.92 = (f32[2,384]{1,0:T(2,128)S(1)}, f32[2,384]{1,0:T(2,128)}, u32[]{:S(2)}) copy-start(f32[2,384]{1,0:T(2,128)} %param.23) | copy-start | bytes 9220
  47.8 29.4 %copy-start.68 = (f32[2,1536]{1,0:T(2,128)S(1)}, f32[2,1536]{1,0:T(2,128)}, u32[]{:S(2)}) copy-start(f32[2,1536]{1,0:T(2,128)} %param.29) | copy-start | bytes 36868
  47.8 30.0 %copy-start.59 = (bf16[2,24,768]{2,1,0:T(8,128)(2,1)S(1)}, bf16[2,24,768]{2,1,0:T(8,128)(2,1)}, u32[]{:S(2)}) copy-start(bf16[2,24,768]{2,1,0:T(8,128)(2,1)} %param.28) | copy-start | bytes 221188
  48.0 29.2 %copy-start.64 = (f32[3,64]{1,0:T(4,128)}, f32[3,64]{1,0:T(4,128)S(1)}, u32[]{:S(2)}) copy-start(f32[3,64]{1,0:T(4,128)S(1)} %add.326) | copy-start | bytes 2308
  66.0 32.2 %copy-start.60 = (bf16[2,768,24]{1,2,0:T(8,128)(2,1)S(1)}, bf16[2,768,24]{1,2,0:T(8,128)(2,1)}, u32[]{:S(2)}) copy-start(bf16[2,768,24]{1,2,0:T(8,128)(2,1)} %param.30) | copy-start | bytes 221188
  66.3 74.7 %copy-start.35 = (bf16[3,64,200]{2,1,0:T(8,128)(2,1)}, bf16[3,64,200]{2,1,0:T(8,128)(2,1)S(1)}, u32[]{:S(2)}) copy-start(bf16[3,64,200]{2,1,0:T(8,128)(2,1)S(1)} %convolution_convert_fusion.11) | copy-start | bytes 230404
  74.2 112.4 %collective-permute-start = (bf16[12,384]{1,0:T(8,128)(2,1)S(1)}, bf16[12,384]{1,0:T(8,128)(2,1)S(1)}, u32[]{:S(2)}, u32[]{:S(2)}) collective-permute-start(bf16[12,384]{1,0:T(8,128)(2,1)S(1)} %slice.160), channel_id=1, source_target_pairs={{0,1},{2,3},{4,5},{6,7},{8,9},{10,11},{12,13},{14,15},{16,17},{18,... | collective-permute-start | bytes 27656
  98.2 98.3 %copy-start = (bf16[1,384,768]{2,1,0:T(8,128)(2,1)}, bf16[1,384,768]{2,1,0:T(8,128)(2,1)S(1)}, u32[]{:S(2)}) copy-start(bf16[1,384,768]{2,1,0:T(8,128)(2,1)S(1)} %all-gather.2) | copy-start | bytes 1769476
  98.3 84.4 %copy-start.93 = (f32[2,384]{1,0:T(2,128)S(1)}, f32[2,384]{1,0:T(2,128)}, u32[]{:S(2)}) copy-start(f32[2,384]{1,0:T(2,128)} %param.27) | copy-start | bytes 9220
  98.3 84.3 %copy-start.94 = (f32[2,384]{1,0:T(2,128)S(1)}, f32[2,384]{1,0:T(2,128)}, u32[]{:S(2)}) copy-start(f32[2,384]{1,0:T(2,128)} %param.26) | copy-start | bytes 9220
  98.3 84.9 %copy-start.51 = (f32[1,100,384]{2,0,1:T(1,128)S(1)}, f32[1,100,384]{2,0,1:T(1,128)}, u32[]{:S(2)}) copy-start(f32[1,100,384]{2,0,1:T(1,128)} %param.17) | copy-start | bytes 460804
  118.9 65.8 %copy-start.95 = (f32[2,384]{1,0:T(2,128)S(1)}, f32[2,384]{1,0:T(2,128)}, u32[]{:S(2)}) copy-start(f32[2,384]{1,0:T(2,128)} %param.31) | copy-start | bytes 9220
  118.9 66.4 %copy-start.106 = (u32[32]{0:T(128)S(1)}, u32[32]{0:T(128)}, u32[]{:S(2)}) copy-start(u32[32]{0:T(128)} %constant.131) | copy-start | bytes 388
  118.9 68.2 %copy-start.17 = (f32[1,100,384]{2,0,1:T(1,128)S(1)}, f32[1,100,384]{2,0,1:T(1,128)}, u32[]{:S(2)}) copy-start(f32[1,100,384]{2,0,1:T(1,128)} %param.16) | copy-start | bytes 460804
  183.2 15.9 %copy-start.69 = (f32[100]{0:T(128)}, f32[100]{0:T(128)S(1)}, u32[]{:S(2)}) copy-start(f32[100]{0:T(128)S(1)} %and_select_fusion) | copy-start | bytes 1204
  199.1 30.2 %copy-start.4 = (bf16[1,3,384,192]{3,2,1,0:T(8,128)(2,1)S(1)}, bf16[1,3,384,192]{3,2,1,0:T(8,128)(2,1)}, u32[]{:S(2)}) copy-start(bf16[1,3,384,192]{3,2,1,0:T(8,128)(2,1)} %all-gather.4) | copy-start | bytes 1327108
  207.3 24.4 %collective-permute-start.1 = (bf16[12,384]{1,0:T(8,128)(2,1)}, bf16[12,384]{1,0:T(8,128)(2,1)}, u32[]{:S(2)}, u32[]{:S(2)}) collective-permute-start(bf16[12,384]{1,0:T(8,128)(2,1)} %slice.161), channel_id=1, source_target_pairs={{0,1},{2,3},{4,5},{6,7},{8,9},{10,11},{12,13},{14,15},{16,17},{18,... | collective-permute-start | bytes 27656
  246.0 17.5 %copy-start.67 = (f32[1,1536]{1,0:T(1,128)S(1)}, f32[1,1536]{1,0:T(1,128)}, u32[]{:S(2)}) copy-start(f32[1,1536]{1,0:T(1,128)} %get-tuple-element.116) | copy-start | bytes 18436
  246.1 18.5 %copy-start.73 = (f32[384]{0:T(512)S(1)}, f32[384]{0:T(512)}, u32[]{:S(2)}) copy-start(f32[384]{0:T(512)} %get-tuple-element.46) | copy-start | bytes 4612
  253.7 10.5 %collective-permute-start.2 = (bf16[12,384]{1,0:T(8,128)(2,1)S(1)}, bf16[12,384]{1,0:T(8,128)(2,1)S(1)}, u32[]{:S(2)}, u32[]{:S(2)}) collective-permute-start(bf16[12,384]{1,0:T(8,128)(2,1)S(1)} %slice.162), channel_id=1, source_target_pairs={{0,1},{2,3},{4,5},{6,7},{8,9},{10,11},{12,13},{14,15},{16,17},{18,... | collective-permute-start | bytes 27656
  279.3 19.2 %copy-start.105 = (f32[100]{0:T(128)S(1)}, f32[100]{0:T(128)}, u32[]{:S(2)}) copy-start(f32[100]{0:T(128)} %copy-done.104) | copy-start | bytes 1204
  279.3 20.8 %copy-start.70 = (f32[100]{0:T(128)S(1)}, f32[100]{0:T(128)}, u32[]{:S(2)}) copy-start(f32[100]{0:T(128)} %copy-done.69) | copy-start | bytes 1204
  289.9 3.4 collective-permute-start.4
  297.0 11.9 %copy-start.10 = (f32[1,1,200,192]{2,3,0,1:T(8,128)S(1)}, f32[1,1,200,192]{2,3,0,1:T(8,128)}, u32[]{:S(2)}) copy-start(f32[1,1,200,192]{2,3,0,1:T(8,128)} %copy-done.9) | copy-start | bytes 460804
  312.3 15.4 %copy-start.88 = (f32[100]{0:T(128)S(1)}, f32[100]{0:T(128)}, u32[]{:S(2)}) copy-start(f32[100]{0:T(128)} %copy-done.87) | copy-start | bytes 1204
  312.3 16.8 %copy-start.103 = (f32[100]{0:T(128)S(1)}, f32[100]{0:T(128)}, u32[]{:S(2)}) copy-start(f32[100]{0:T(128)} %copy-done.102) | copy-start | bytes 1204
  321.1 3.3 collective-permute-start.5
  347.8 5.6 collective-permute-start.6
  351.8 111.9 %reduce-scatter.31.cloned.1.call-start = ((), (), s32[]{:S(2)}) async-start(), calls=%async_computation.6 | async-start | bytes 417792 | tf_op jit(solution)/shard_map/reduce_scatter | solution.py:274
  366.2 203.7 %all-reduce.23.cloned.1.call-start = ((), (), s32[]{:S(2)}) async-start(), calls=%async_computation.12 | async-start | bytes 6291456
  368.8 262.0 %reduce-scatter.41.cloned.1.call-start = ((), (), s32[]{:S(2)}) async-start(), calls=%async_computation.11 | async-start | bytes 1253376 | tf_op jit(solution)/shard_map/reduce_scatter | solution.py:276
  371.2 320.1 %reduce-scatter.39.cloned.1.call-start = ((), (), s32[]{:S(2)}) async-start(), calls=%async_computation.10 | async-start | bytes 1253376 | tf_op jit(solution)/shard_map/reduce_scatter | solution.py:276
  372.8 379.1 %reduce-scatter.37.cloned.1.call-start = ((), (), s32[]{:S(2)}) async-start(), calls=%async_computation.9 | async-start | bytes 1253376 | tf_op jit(solution)/shard_map/reduce_scatter | solution.py:275
  374.4 438.2 %reduce-scatter.35.cloned.1.call-start = ((), (), s32[]{:S(2)}) async-start(), calls=%async_computation.8 | async-start | bytes 1253376 | tf_op jit(solution)/shard_map/reduce_scatter | solution.py:275
  378.2 12.0 %copy-start.84 = (f32[100]{0:T(128)S(1)}, f32[100]{0:T(128)}, u32[]{:S(2)}) copy-start(f32[100]{0:T(128)} %copy-done.83) | copy-start | bytes 1204
  378.2 53.5 %copy-start.99 = (f32[100]{0:T(128)S(1)}, f32[100]{0:T(128)}, u32[]{:S(2)}) copy-start(f32[100]{0:T(128)} %copy-done.98) | copy-start | bytes 1204
  378.6 55.5 %copy-start.19 = (f32[1,100,384]{2,0,1:T(1,128)S(1)}, f32[1,100,384]{2,0,1:T(1,128)}, u32[]{:S(2)}) copy-start(f32[1,100,384]{2,0,1:T(1,128)} %copy-done.18) | copy-start | bytes 460804
  378.7 55.5 %copy-start.71 = (f32[100]{0:T(128)S(1)}, f32[100]{0:T(128)}, u32[]{:S(2)}) copy-start(f32[100]{0:T(128)} %copy-done.69) | copy-start | bytes 1204
  378.7 55.5 %copy-start.72 = (f32[384]{0:T(512)S(1)}, f32[384]{0:T(512)}, u32[]{:S(2)}) copy-start(f32[384]{0:T(512)} %get-tuple-element.40) | copy-start | bytes 4612
  386.0 3.7 collective-permute-start.7
  388.2 3.1 collective-permute-start.3
  (77 other events, 299.5 us)
Sparse Core Ops, SparseCore 0:
  351.8 53.2 reduce-scatter.32
  409.0 54.5 reduce-scatter.30
  467.3 102.5 all-reduce.22
  573.4 57.2 reduce-scatter.40
  634.2 57.1 reduce-scatter.38
  694.8 57.0 reduce-scatter.36
  755.5 57.0 reduce-scatter.34
where the time goes:
time: 823 us; the launch traced here: 821 us
  waiting for transfers between devices  373 us (45%)
  blocking collectives  308 us (37%)
  other arithmetic  38.4 us (5%)
  local copies, waits for them, and re-layouts  34.7 us (4%)
  matrix products  27.8 us (3%)
  starting transfers between devices  20.3 us (2%)
  between operations  18.4 us (2%)
    reduce_scatter x2, waiting for transfers between devices, local(): lax.psum_scatter(up_grad, 'fsdp', scatter_dimension=0, tiled=True)  120 us
    reduce_scatter x2, waiting for transfers between devices, local(): lax.psum_scatter(down_grad, 'fsdp', scatter_dimension=1, tiled=True)  119 us
    unnamed x16, waiting for transfers between devices  106 us
    unnamed x7, blocking collectives  52.9 us
    all_gather x2, blocking collectives, fetch_weights(): lax.all_gather(qkv_part, 'fsdp', axis=1, tiled=True)  45.8 us
    all_gather x2, blocking collectives, fetch_weights(): lax.all_gather(down_part, 'fsdp', axis=1, tiled=True)  41.2 us
    all_gather x2, blocking collectives, fetch_weights(): lax.all_gather(up_part, 'fsdp', axis=0, tiled=True)  40.8 us
    psum x1, blocking collectives, local(): lax.psum((small_stacked[0], small_stacked[1], small_stacked[2], small_sta...  39.9 us
  transfers between devices with their start and end apart: 15, of which 7 were waited for; matrix products, arithmetic and copies ran while one was open for 6% of the time, Pallas kernels for 0%

commit v1 on v0

--- a/solution.py
+++ b/solution.py
@@ -3,6 +3,8 @@
 import jax
 import jax.numpy as jnp
 from jax import lax
+from jax.experimental import pallas as pl
+from jax.experimental.pallas import tpu as pltpu
 from jax.sharding import PartitionSpec as P
 
 D = 384
@@ -328,6 +330,461 @@
     )
 
 
+BF = jnp.bfloat16
+F32 = jnp.float32
+HALF = 112
+ROWS = 2 * HALF
+WIDE = 1280
+FFN = pl.ds(0, 768)
+ATT = pl.ds(768, 512)
+PARTS = (FFN, ATT)
+COPIES = 82
+
+
+def dot(a, b, ca, cb):
+    return lax.dot_general(a, b, (((ca,), (cb,)), ((), ())), preferred_element_type=F32)
+
+
+def row_stats(x):
+    centre = x - jnp.mean(x, axis=-1, keepdims=True)
+    r = lax.rsqrt(jnp.mean(centre * centre, axis=-1, keepdims=True) + epsilon)
+    return centre * r, r
+
+
+def norm_grad(e, xhat, r, gain):
+    gy = e * gain
+    return r * (
+        gy
+        - jnp.mean(gy, axis=-1, keepdims=True)
+        - xhat * jnp.mean(gy * xhat, axis=-1, keepdims=True)
+    )
+
+
+def col_sum(x):
+    return jnp.sum(x, axis=0, keepdims=True)
+
+
+def fused_kernel(
+    count_ref, valid_ref, img_ref, ups_ref, pack_ref, vec_ref, qvb_ref, upb_ref,
+    out_ref, gimg_ref, gw_ref, small_ref,
+    w_ref, pr_ref, hid_ref, mid_ref, g_ref, n1_ref, n2_ref, q_ref, k_ref, v_ref, p_ref,
+    mix_ref, act_ref, dg_ref, xs_ref, xr_ref, gs_ref, r1_ref, s1_ref, r2_ref, s2_ref,
+    r3_ref, s3_ref, sm_ref, smr_ref, smz_ref, send_sem, recv_sem,
+):
+    f = lax.axis_index("fsdp")
+    x = lax.axis_index("tensor")
+    c = lax.rem(f, 2)
+    y = lax.rem(f // 2, 2)
+    z = f // 4
+
+    def at(zz, yy, cc):
+        return {"fsdp": zz * 4 + yy * 2 + cc}
+
+    core_peer = at(z, y, 1 - c)
+    y_peer = at(z, 1 - y, c)
+    x_peer = {"tensor": 1 - x}
+    z_next = [lax.rem(z + d, 4) for d in range(4)]
+    z_from = [lax.rem(z + 4 - d, 4) for d in range(4)]
+
+    barrier = pltpu.get_barrier_semaphore()
+    greeted = [core_peer, y_peer, x_peer] + [at(z_next[d], y, c) for d in (1, 2, 3)]
+    for peer in greeted:
+        pl.semaphore_signal(barrier, inc=1, device_id=peer, device_id_type=pl.DeviceIdType.MESH)
+    pl.semaphore_wait(barrier, len(greeted))
+
+    started = []
+
+    def send(src, dst, peer):
+        i = len(started)
+        copy = pltpu.make_async_remote_copy(
+            src_ref=src, dst_ref=dst, send_sem=send_sem.at[i], recv_sem=recv_sem.at[i],
+            device_id=peer, device_id_type=pl.DeviceIdType.MESH,
+        )
+        copy.start()
+        started.append(copy)
+        return copy
+
+    pack_copies = [send(pack_ref.at[l, 1 - c], pr_ref.at[l], core_peer) for l in range(2)]
+
+    own_row = lax.broadcasted_iota(jnp.int32, (HALF, 1), 0)
+    valid = valid_ref[0]
+    own_ok = (own_row < 100) & (x * 100 + own_row < valid) & (count_ref[0] > 0)
+    row_ok = jnp.where(own_ok, 1.0, 0.0).astype(F32)
+    hid_ref[0, 96:HALF] = jnp.zeros((HALF - 96, 384), F32)
+    hid_ref[0, 0:100] = img_ref[...]
+    img_copy = send(hid_ref.at[0, 0:HALF], hid_ref.at[0, HALF:ROWS], x_peer)
+
+    z_copies, y_copies, c_copies = {}, {}, {}
+    for l in range(2):
+        pack_copies[l].wait_recv()
+        mine = pack_ref[l, c].astype(F32)[:24]
+        theirs = pr_ref[l].astype(F32)[:24]
+        first = jnp.broadcast_to(c, mine.shape) == 0
+        chunk = jnp.concatenate(
+            [jnp.where(first, mine, theirs), jnp.where(first, theirs, mine)], axis=0
+        )
+        w_ref[l, c, z, y] = chunk.astype(BF)
+        for a in (1, 0):
+            block = w_ref.at[l, c, z, y, :, PARTS[a]]
+            z_copies[l, a] = [send(block, block, at(z_next[d], y, c)) for d in (1, 2, 3)]
+            y_copies[l, a] = [send(block, block, y_peer)]
+
+    g_ref[96:HALF] = jnp.zeros((HALF - 96, 384), F32)
+    g_ref[0:100] = ups_ref[...]
+    g_ref[0:HALF] = g_ref[0:HALF] * row_ok
+    ups_copy = send(g_ref.at[0:HALF], g_ref.at[HALF:ROWS], x_peer)
+
+    def gather_y(l, a):
+        for d in (1, 2, 3):
+            z_copies[l, a][d - 1].wait_recv()
+            block = w_ref.at[l, c, z_from[d], y, :, PARTS[a]]
+            y_copies[l, a].append(send(block, block, y_peer))
+
+    def gather_core(l, a):
+        for copy in y_copies[l, a]:
+            copy.wait_recv()
+        block = w_ref.at[l, c, :, :, :, PARTS[a]]
+        c_copies[l, a] = send(block, block, core_peer)
+
+    def gather_end(l, a):
+        c_copies[l, a].wait_recv()
+
+    def x_start(i, value):
+        xs_ref[i] = value.astype(BF)
+        return [
+            send(xs_ref.at[i, HALF:ROWS], xr_ref.at[i, 0:HALF], x_peer),
+            send(xs_ref.at[i, 0:HALF], xr_ref.at[i, HALF:ROWS], x_peer),
+        ]
+
+    def x_end(i, copies):
+        for copy in copies:
+            copy.wait_recv()
+        return xs_ref[i].astype(F32) + xr_ref[i].astype(F32)
+
+    def weight(l, half, start, size):
+        return w_ref[l, half, :, :, :, pl.ds(start, size)].reshape(384, size)
+
+    def vec(l, i):
+        return vec_ref[l, i : i + 1]
+
+    lane = lax.broadcasted_iota(jnp.int32, (ROWS, 256), 1)
+    head_mask = [
+        jnp.where((lane >= HD * h) & (lane < HD * h + HD), 1.0, 0.0).astype(F32).astype(BF)
+        for h in range(3)
+    ]
+    key = lax.broadcasted_iota(jnp.int32, (ROWS, ROWS), 1)
+    in_half = jnp.where(key < HALF, key, key - HALF)
+    token = in_half + 100 * jnp.where(key < HALF, x, 1 - x)
+    key_ok = (in_half < 100) & (token < valid)
+
+    def attention(l):
+        xhat, r = row_stats(hid_ref[l])
+        n1 = (xhat * vec(l, 1) + vec(l, 2)).astype(BF)
+        n1_ref[l] = n1
+        yield
+        q = (dot(n1, weight(l, 0, 1024, 256), 1, 0) + qvb_ref[l, 0:1]).astype(BF)
+        k = dot(n1, weight(l, 1, 768, 256), 1, 0).astype(BF)
+        v = (dot(n1, weight(l, 1, 1024, 256), 1, 0) + qvb_ref[l, 1:2]).astype(BF)
+        q_ref[l], k_ref[l], v_ref[l] = q, k, v
+        mixed = jnp.zeros((ROWS, 256), F32)
+        for h in range(3):
+            scores = jnp.where(key_ok, dot(q * head_mask[h], k, 1, 1) * HD ** (-0.5), -1e30)
+            e = jnp.exp(scores - jnp.max(scores, axis=-1, keepdims=True))
+            p = e / jnp.sum(e, axis=-1, keepdims=True)
+            p_ref[l, h] = p
+            mixed = mixed + dot(p.astype(BF), v * head_mask[h], 1, 0)
+        mix_ref[l] = mixed.astype(BF)
+        copies = x_start(2 * l, dot(mix_ref[l], weight(l, 0, 768, 256), 1, 1))
+        yield
+        branch = x_end(2 * l, copies)
+        mid_ref[l] = hid_ref[l] + (branch + vec(l, 0))
+
+    def feed(l):
+        xhat, r = row_stats(mid_ref[l])
+        n2 = (xhat * vec(l, 3) + vec(l, 4)).astype(BF)
+        n2_ref[l] = n2
+        yield
+        up = dot(n2, weight(l, 0, 0, 768), 1, 0) + upb_ref[l]
+        phi = 0.5 * (1.0 + lax.erf(up * (0.5**0.5)))
+        act_ref[l] = (up * phi).astype(BF)
+        dg_ref[l] = phi + up * (jnp.exp(-0.5 * up * up) * 0.3989422804014327)
+        copies = x_start(2 * l + 1, dot(act_ref[l], weight(l, 1, 0, 768), 1, 1))
+        yield
+        branch = x_end(2 * l + 1, copies)
+        hid_ref[l + 1] = mid_ref[l] + (branch + vec(l, 5))
+
+    gather_y(0, 1)
+    gather_y(0, 0)
+    img_copy.wait_recv()
+    step = attention(0)
+    next(step)
+    gather_core(0, 1)
+    gather_end(0, 1)
+    next(step)
+    gather_core(0, 0)
+    gather_y(1, 1)
+    next(step, None)
+    step = feed(0)
+    next(step)
+    gather_end(0, 0)
+    next(step)
+    gather_core(1, 1)
+    gather_y(1, 0)
+    next(step, None)
+    step = attention(1)
+    next(step)
+    gather_end(1, 1)
+    next(step)
+    gather_core(1, 0)
+    next(step, None)
+    step = feed(1)
+    next(step)
+    gather_end(1, 0)
+    next(step)
+    next(step, None)
+    out_ref[...] = (hid_ref[2, 0:HALF] * row_ok)[0:100]
+    ups_copy.wait()
+
+    unit = {}
+
+    def reduce_core(l, a):
+        part = PARTS[a]
+        unit[l, a] = [
+            send(gs_ref.at[l, 1 - c, :, :, :, part], r1_ref.at[l, :, :, :, part], core_peer)
+        ]
+
+    def reduce_y(l, a):
+        part = PARTS[a]
+        unit[l, a][0].wait_recv()
+        total = gs_ref[l, c, :, :, :, part].astype(F32) + r1_ref[l, :, :, :, part].astype(F32)
+        s1_ref[l, :, :, :, part] = total.astype(BF)
+        unit[l, a] = [send(s1_ref.at[l, :, 1 - y, :, part], r2_ref.at[l, :, :, part], y_peer)]
+
+    def reduce_z(l, a):
+        part = PARTS[a]
+        unit[l, a][0].wait_recv()
+        total = s1_ref[l, :, y, :, part].astype(F32) + r2_ref[l, :, :, part].astype(F32)
+        s2_ref[l, :, :, part] = total.astype(BF)
+        unit[l, a] = [
+            send(
+                s2_ref.at[l, z_next[d], :, part], r3_ref.at[l, d - 1, :, part],
+                at(z_next[d], y, c),
+            )
+            for d in (1, 2, 3)
+        ]
+
+    def reduce_last(l, a):
+        part = PARTS[a]
+        for copy in unit[l, a]:
+            copy.wait_recv()
+        total = s2_ref[l, z, :, part].astype(F32)
+        for d in range(3):
+            total = total + r3_ref[l, d, :, part].astype(F32)
+        s3_ref[l, :, part] = total
+        other = pl.ds(pl.multiple_of(24 * (1 - c), 8), 24)
+        own = pl.ds(pl.multiple_of(24 * c, 8), 24)
+        unit[l, a] = [send(s3_ref.at[l, other, part], gw_ref.at[l, c, :, part], core_peer)]
+        gw_ref[l, c, :, part] = s3_ref[l, own, part]
+
+    def keep(l, half, start, value):
+        size = value.shape[1]
+        gs_ref[l, half, :, :, :, pl.ds(start, size)] = value.astype(BF).reshape(4, 2, 48, size)
+
+    def feed_back(l):
+        g = g_ref[...]
+        gb = g.astype(BF)
+        ga = dot(gb, weight(l, 1, 0, 768), 1, 0)
+        gu = (ga * dg_ref[l]).astype(BF)
+        copies = x_start(6 - 2 * l, dot(gu, weight(l, 0, 0, 768), 1, 1))
+        keep(l, 1, 0, dot(gb, act_ref[l], 0, 0))
+        keep(l, 0, 0, dot(n2_ref[l], gu, 0, 0))
+        reduce_core(l, 0)
+        yield
+        sm_ref[0, 8 * l : 8 * l + 1, :] = col_sum(gu.astype(F32))
+        sm_ref[0, 8 * l + 4 : 8 * l + 5, 384:768] = col_sum(gb.astype(F32))
+        xhat, r = row_stats(mid_ref[l])
+        e = x_end(6 - 2 * l, copies)
+        sm_ref[0, 8 * l + 3 : 8 * l + 4, 384:768] = col_sum(e * xhat)
+        sm_ref[0, 8 * l + 4 : 8 * l + 5, 0:384] = col_sum(e)
+        g_ref[...] = g + norm_grad(e, xhat, r, vec(l, 3))
+
+    def attention_back(l):
+        g = g_ref[...]
+        gm = g.astype(BF)
+        q, k, v = q_ref[l], k_ref[l], v_ref[l]
+        gmix = dot(gm, weight(l, 0, 768, 256), 1, 0).astype(BF)
+        gq = jnp.zeros((ROWS, 256), F32)
+        gk, gv = gq, gq
+        for h in range(3):
+            p = p_ref[l, h]
+            gmh = gmix * head_mask[h]
+            dp = dot(gmh, v, 1, 1)
+            gv = gv + dot(p.astype(BF), gmh, 0, 0)
+            ds = (p * (dp - jnp.sum(p * dp, axis=-1, keepdims=True))).astype(BF)
+            gq = gq + dot(ds, k * head_mask[h], 1, 0)
+            gk = gk + dot(ds, q * head_mask[h], 0, 0)
+        gq = (gq * HD ** (-0.5)).astype(BF)
+        gk = (gk * HD ** (-0.5)).astype(BF)
+        gv = gv.astype(BF)
+        copies = x_start(
+            7 - 2 * l,
+            dot(gq, weight(l, 0, 1024, 256), 1, 1)
+            + dot(gk, weight(l, 1, 768, 256), 1, 1)
+            + dot(gv, weight(l, 1, 1024, 256), 1, 1),
+        )
+        n1 = n1_ref[l]
+        keep(l, 0, 768, dot(gm, mix_ref[l], 0, 0))
+        keep(l, 0, 1024, dot(n1, gq, 0, 0))
+        keep(l, 1, 768, dot(n1, gk, 0, 0))
+        keep(l, 1, 1024, dot(n1, gv, 0, 0))
+        reduce_core(l, 1)
+        yield
+        sm_ref[0, 8 * l + 1 : 8 * l + 2, 0:256] = col_sum(gq.astype(F32))
+        sm_ref[0, 8 * l + 1 : 8 * l + 2, 256:512] = col_sum(gv.astype(F32))
+        sm_ref[0, 8 * l + 2 : 8 * l + 3, 0:384] = col_sum(gm.astype(F32))
+        xhat, r = row_stats(hid_ref[l])
+        e = x_end(7 - 2 * l, copies)
+        sm_ref[0, 8 * l + 2 : 8 * l + 3, 384:768] = col_sum(e * xhat)
+        sm_ref[0, 8 * l + 3 : 8 * l + 4, 0:384] = col_sum(e)
+        g_ref[...] = g + norm_grad(e, xhat, r, vec(l, 1))
+
+    sm_ref[0] = jnp.zeros((16, 768), F32)
+    step = feed_back(1)
+    next(step)
+    next(step, None)
+    step = attention_back(1)
+    next(step)
+    reduce_y(1, 0)
+    next(step, None)
+    step = feed_back(0)
+    next(step)
+    reduce_z(1, 0)
+    reduce_y(1, 1)
+    next(step, None)
+    step = attention_back(0)
+    next(step)
+    reduce_y(0, 0)
+    reduce_z(1, 1)
+    reduce_last(1, 0)
+    next(step, None)
+
+    small = send(sm_ref.at[0], smr_ref.at[0], core_peer)
+    reduce_y(0, 1)
+    gimg_ref[...] = g_ref[0:HALF][0:100]
+    small.wait_recv()
+    sm_ref[1] = sm_ref[0] + smr_ref[0]
+    small = send(sm_ref.at[1], smr_ref.at[1], y_peer)
+    reduce_z(0, 0)
+    reduce_last(1, 1)
+    small.wait_recv()
+    smz_ref[z] = sm_ref[1] + smr_ref[1]
+    smalls = [send(smz_ref.at[z], smz_ref.at[z], at(z_next[d], y, c)) for d in (1, 2, 3)]
+    reduce_z(0, 1)
+    reduce_last(0, 0)
+    for small in smalls:
+        small.wait_recv()
+    small_ref[x] = ((smz_ref[0] + smz_ref[1]) + smz_ref[2]) + smz_ref[3]
+    small = send(small_ref.at[x], small_ref.at[x], x_peer)
+    reduce_last(0, 1)
+    for copies in unit.values():
+        for copy in copies:
+            copy.wait_recv()
+    small.wait_recv()
+    for copy in started:
+        if copy is not ups_copy:
+            copy.wait_send()
+
+
+def fused_local(
+    images, upstream, image_count, valid_tokens, qkv_weight, qv_bias, out_weight, out_bias,
+    gain_one, shift_one, gain_two, shift_two, up_weight, up_bias, down_weight, down_bias,
+):
+    rank = lax.axis_index("tensor")
+    pad = lambda a: jnp.pad(a, [(0, 0)] * (a.ndim - 1) + [(0, 64)])
+    turn = lambda a: jnp.swapaxes(a, 1, 2)
+    pack = jnp.stack(
+        [
+            jnp.concatenate(
+                [up_weight, pad(turn(out_weight)), pad(qkv_weight[:, 0])], axis=-1
+            ),
+            jnp.concatenate(
+                [turn(down_weight), pad(qkv_weight[:, 1]), pad(qkv_weight[:, 2])], axis=-1
+            ),
+        ],
+        axis=1,
+    )
+    pack = jnp.pad(pack, [(0, 0), (0, 0), (0, 8), (0, 0)])
+    vecs = jnp.stack(
+        [out_bias, gain_one, shift_one, gain_two, shift_two, down_bias, out_bias, out_bias], axis=1
+    )
+    qvb = pad(take_half(qv_bias, 192, rank))
+    upb = take_half(up_bias, 768, rank)[:, None]
+    vmem = pl.BlockSpec(memory_space=pltpu.VMEM)
+    smem = pl.BlockSpec(memory_space=pltpu.SMEM)
+    V = pltpu.VMEM
+    output, grad_images, grads, small = pl.pallas_call(
+        fused_kernel,
+        out_shape=(
+            jax.ShapeDtypeStruct((100, 384), F32),
+            jax.ShapeDtypeStruct((100, 384), F32),
+            jax.ShapeDtypeStruct((2, 2, 24, WIDE), F32),
+            jax.ShapeDtypeStruct((2, 16, 768), F32),
+        ),
+        in_specs=[smem] * 2 + [vmem] * 6,
+        out_specs=(vmem,) * 4,
+        scratch_shapes=[
+            V((2, 2, 4, 2, 48, WIDE), BF),
+            V((2, 32, WIDE), BF),
+            V((3, ROWS, 384), F32),
+            V((2, ROWS, 384), F32),
+            V((ROWS, 384), F32),
+            V((2, ROWS, 384), BF),
+            V((2, ROWS, 384), BF),
+            V((2, ROWS, 256), BF),
+            V((2, ROWS, 256), BF),
+            V((2, ROWS, 256), BF),
+            V((2, 3, ROWS, ROWS), F32),
+            V((2, ROWS, 256), BF),
+            V((2, ROWS, 768), BF),
+            V((2, ROWS, 768), F32),
+            V((8, ROWS, 384), BF),
+            V((8, ROWS, 384), BF),
+            V((2, 2, 4, 2, 48, WIDE), BF),
+            V((2, 4, 2, 48, WIDE), BF),
+            V((2, 4, 2, 48, WIDE), BF),
+            V((2, 4, 48, WIDE), BF),
+            V((2, 4, 48, WIDE), BF),
+            V((2, 3, 48, WIDE), BF),
+            V((2, 48, WIDE), F32),
+            V((2, 16, 768), F32),
+            V((2, 16, 768), F32),
+            V((4, 16, 768), F32),
+            pltpu.SemaphoreType.DMA((COPIES,)),
+            pltpu.SemaphoreType.DMA((COPIES,)),
+        ],
+        compiler_params=pltpu.CompilerParams(
+            collective_id=0, has_side_effects=True, vmem_limit_bytes=48 * 2**20
+        ),
+        cost_estimate=pl.CostEstimate(
+            flops=3 * 10**9, bytes_accessed=2 * 10**7, transcendentals=10**6
+        ),
+    )(image_count, valid_tokens, images[0], upstream[0], pack, vecs, qvb, upb)
+    up_grad = grads[:, 0, :, 0:768]
+    out_grad = turn(grads[:, 0, :, 768:960])
+    down_grad = turn(grads[:, 1, :, 0:768])
+    qkv_grad = jnp.stack(
+        [grads[:, 0, :, 1024:1216], grads[:, 1, :, 768:960], grads[:, 1, :, 1024:1216]], axis=1
+    )
+    small = small.reshape(2, 2, 8, 768)
+    up_bias_grad = jnp.concatenate([small[0, :, 0], small[1, :, 0]], axis=-1)
+    qv = small[:, :, 1, 0:512].reshape(2, 2, 2, 256)[..., 0:192]
+    qv_bias_grad = jnp.concatenate([qv[0], qv[1]], axis=-1)
+    row = lambda i, side: small[0, :, i, 384 * side : 384 * side + 384]
+    return (
+        output[None], grad_images[None], qkv_grad, qv_bias_grad, out_grad, row(2, 0),
+        row(2, 1), row(3, 0), row(3, 1), row(4, 0), up_grad, up_bias_grad, down_grad, row(4, 1),
+    )
+
 def solution(mesh):
     in_specs = (
         P("fsdp", "tensor", None),
@@ -363,4 +820,5 @@
         P(None, "tensor", "fsdp"),
         P(),
     )
-    return jax.shard_map(local, mesh=mesh, in_specs=in_specs, out_specs=out_specs, check_vma=False)
+    body = fused_local if mesh.shape["fsdp"] == 16 else local
+    return jax.shard_map(body, mesh=mesh, in_specs=in_specs, out_specs=out_specs, check_vma=False)

time: 823 us -> 107 us (0.13)
  waiting for transfers between devices: 373 us -> 0 us
  blocking collectives: 308 us -> 0 us
  Pallas kernels: 0 us -> 93.7 us
  other arithmetic: 38.4 us -> 2 us
  matrix products: 27.8 us -> 0 us
  local copies, waits for them, and re-layouts: 34.7 us -> 8.68 us
  starting transfers between devices: 20.3 us -> 0 us
  between operations: 18.4 us -> 2.27 us
    reduce_scatter x6 -> x0, waiting for transfers between devices: 267 us -> none  [the longest x2 120 us: local(): lax.psum_scatter(up_grad, 'fsdp', scatter_dimension=0, tiled=True)]
    all_gather x16 -> x0, blocking collectives: 216 us -> none  [the longest x2 45.8 us: fetch_weights(): lax.all_gather(qkv_part, 'fsdp', axis=1, tiled=True)]
    unnamed x16 -> x0, waiting for transfers between devices: 106 us -> none
    pallas_call x0 -> x1, Pallas kernels: none -> 93.7 us  [fused_local(): pl.pallas_call(fused_kernel, out_shape=(jax.ShapeDtypeStruct((100, 384),...]
    unnamed x7 -> x0, blocking collectives: 52.9 us -> none
    psum x1 -> x0, blocking collectives: 39.9 us -> none  [local(): lax.psum((small_stacked[0], small_stacked[1], small_stacked[2], small_sta...]
    reduce_sum x22 -> x0, other arithmetic: 28.2 us -> none  [the longest x8 12.4 us: norm_rows(): centre = hidden - jnp.mean(hidden, axis=-1, keepdims=True)]
    dot_general x34 -> x0, matrix products: 27.2 us -> none  [the longest x2 5.92 us: local(): jnp.einsum('std,df->stf', shared_two, up_full, preferred_element_type=jnp...]
  transfers between devices with their start and end apart: 15 -> 0, of which waited for: 7 -> 0; matrix products, arithmetic and copies ran while one was open for 6% -> 0% of each run, Pallas kernels for 0% -> 0%
where the time goes in v1:
time: 107 us
  Pallas kernels  93.7 us (88%)
  local copies, waits for them, and re-layouts  8.68 us (8%)
  between operations  2.27 us (2%)
  other arithmetic  2 us (2%)
    pallas_call x1, Pallas kernels, fused_local(): pl.pallas_call(fused_kernel, out_shape=(jax.ShapeDtypeStruct((100, 384),...  93.7 us
    unnamed x39, local copies, waits for them, and re-layouts  7.04 us

profile of v1, /device:TPU:0, one launch (start us, length us, event | category | flops | bytes accessed | tf_op | source)
XLA Modules:
  0.0 106.7 jit_solution(14369615925861461822)
XLA Ops:
  0.6 0.0 copy-start
  0.7 0.0 copy-start.7
  0.7 0.0 copy-start.8
  0.7 0.0 copy-start.9
  0.7 0.0 copy-start.10
  0.7 0.0 copy-start.11
  0.7 0.0 copy-start.12
  0.7 0.0 copy-start.13
  0.7 0.0 copy-start.3
  2.1 0.0 copy-done.7
  2.1 0.0 copy-done.8
  2.1 0.0 copy-done.9
  2.1 0.0 copy-done.10
  2.2 0.0 copy-done.11
  2.2 0.0 copy-done.12
  2.2 0.0 copy-done.13
  2.2 0.1 constant_dynamic-slice_fusion.1
  2.3 0.0 copy-done
  2.3 0.0 copy-start.6
  2.4 0.1 stack.44.vec_ref
  2.4 0.0 copy-done.3
  2.4 0.0 copy-start.4
  2.4 0.0 copy-start.5
  2.5 0.6 copy-done.6
  3.1 0.2 copy-done.4
  3.3 0.0 copy-done.5
  3.4 0.0 copy-start.1
  3.4 0.0 copy-start.2
  3.4 0.9 copy-done.1
  4.3 0.1 copy-done.2
  4.4 93.7 %shard_map.263 = (f32[100,384]{1,0:T(8,128)S(1)}, f32[100,384]{1,0:T(8,128)S(1)}, f32[2,2,24,1280]{3,2,1,0:T(8,128)S(1)}, f32[2,16,768]{2,1,0:T(8,128)S(1)}) custom-call(s32[1]{0:T(128)S(6)} %copy.74.count_ref, s32[1]{0:T(128)S(6)} %copy.75.valid_ref, f32[100,384]{1,0:T(8,128)S(1)} %get-tuple-element.58.img_ref, f32[100,384]{1,0:T(8,128)S(1)} %get-tuple-element.57.ups_ref, ...), custom_call_target="tpu_custom_call" | custom-call | flops 3000000000 | bytes 20000000 | tf_op jit(solution)/shard_map/pallas_call | solution.py:725
  98.2 0.8 copy.41
  99.0 0.8 copy.42
  99.9 0.7 pad_maximum_fusion.2
  100.6 0.6 copy.68
  101.2 0.6 copy.69
  101.7 0.6 copy.70
  102.3 0.6 copy.71
  102.9 0.6 copy.72
  103.5 0.6 copy.73
  104.1 0.6 pad_maximum_fusion.1
  104.7 0.6 slice_bitcast_fusion.2
  105.3 0.7 slice_bitcast_fusion
  106.0 0.7 pad_maximum_fusion
  (20 shorter events, 0.2 us)
Async XLA Ops:
  0.6 1.7 %copy-start = (f32[2,1536]{1,0:T(2,128)S(1)}, f32[2,1536]{1,0:T(2,128)}, u32[]{:S(2)}) copy-start(f32[2,1536]{1,0:T(2,128)} %param.29) | copy-start | bytes 36868
  0.7 1.4 %copy-start.7 = (f32[2,384]{1,0:T(2,128)S(1)}, f32[2,384]{1,0:T(2,128)}, u32[]{:S(2)}) copy-start(f32[2,384]{1,0:T(2,128)} %param.23) | copy-start | bytes 9220
  0.7 1.4 %copy-start.8 = (f32[2,384]{1,0:T(2,128)S(1)}, f32[2,384]{1,0:T(2,128)}, u32[]{:S(2)}) copy-start(f32[2,384]{1,0:T(2,128)} %param.24) | copy-start | bytes 9220
  0.7 1.4 %copy-start.9 = (f32[2,384]{1,0:T(2,128)S(1)}, f32[2,384]{1,0:T(2,128)}, u32[]{:S(2)}) copy-start(f32[2,384]{1,0:T(2,128)} %param.25) | copy-start | bytes 9220
  0.7 1.4 %copy-start.10 = (f32[2,384]{1,0:T(2,128)S(1)}, f32[2,384]{1,0:T(2,128)}, u32[]{:S(2)}) copy-start(f32[2,384]{1,0:T(2,128)} %param.26) | copy-start | bytes 9220
  0.7 1.5 %copy-start.11 = (f32[2,384]{1,0:T(2,128)S(1)}, f32[2,384]{1,0:T(2,128)}, u32[]{:S(2)}) copy-start(f32[2,384]{1,0:T(2,128)} %param.27) | copy-start | bytes 9220
  0.7 1.5 %copy-start.12 = (f32[2,384]{1,0:T(2,128)S(1)}, f32[2,384]{1,0:T(2,128)}, u32[]{:S(2)}) copy-start(f32[2,384]{1,0:T(2,128)} %param.31) | copy-start | bytes 9220
  0.7 1.5 %copy-start.13 = (f32[2,2,384]{2,1,0:T(2,128)S(1)}, f32[2,2,384]{2,1,0:T(2,128)}, u32[]{:S(2)}) copy-start(f32[2,2,384]{2,1,0:T(2,128)} %param.21) | copy-start | bytes 18436
  0.7 1.7 %copy-start.3 = (bf16[2,3,24,192]{3,2,1,0:T(8,128)(2,1)S(1)}, bf16[2,3,24,192]{3,2,1,0:T(8,128)(2,1)}, u32[]{:S(2)}) copy-start(bf16[2,3,24,192]{3,2,1,0:T(8,128)(2,1)} %param.20) | copy-start | bytes 165892
  2.3 0.7 copy-start.6
  2.4 0.9 copy-start.4
  2.4 0.9 copy-start.5
  3.4 0.9 copy-start.1
  3.4 1.0 copy-start.2

commit v2 on v1

--- a/solution.py
+++ b/solution.py
@@ -338,7 +338,7 @@
 FFN = pl.ds(0, 768)
 ATT = pl.ds(768, 512)
 PARTS = (FFN, ATT)
-COPIES = 82
+COPIES = 90
 
 
 def dot(a, b, ca, cb):
@@ -366,8 +366,9 @@
 
 def fused_kernel(
     count_ref, valid_ref, img_ref, ups_ref, pack_ref, vec_ref, qvb_ref, upb_ref,
-    out_ref, gimg_ref, gw_ref, small_ref,
-    w_ref, pr_ref, hid_ref, mid_ref, g_ref, n1_ref, n2_ref, q_ref, k_ref, v_ref, p_ref,
+    out_ref, gimg_ref, gw_ref, small_ref, late_sum_ref,
+    late_ref, late_out_ref,
+    own_ref, tok_ref, w_ref, pr_ref, hid_ref, mid_ref, g_ref, n1_ref, n2_ref, q_ref, k_ref, v_ref, p_ref,
     mix_ref, act_ref, dg_ref, xs_ref, xr_ref, gs_ref, r1_ref, s1_ref, r2_ref, s2_ref,
     r3_ref, s3_ref, sm_ref, smr_ref, smz_ref, send_sem, recv_sem,
 ):
@@ -388,6 +389,9 @@
 
     barrier = pltpu.get_barrier_semaphore()
     greeted = [core_peer, y_peer, x_peer] + [at(z_next[d], y, c) for d in (1, 2, 3)]
+    over_zx = [x_peer] + [{**at(z_next[d], y, c), "tensor": t} for d in (1, 2, 3) for t in (x, 1 - x)]
+    over_yc = [core_peer, y_peer, at(z, 1 - y, 1 - c)]
+    greeted += over_zx[2::2] + over_yc[2:]
     for peer in greeted:
         pl.semaphore_signal(barrier, inc=1, device_id=peer, device_id_type=pl.DeviceIdType.MESH)
     pl.semaphore_wait(barrier, len(greeted))
@@ -410,9 +414,12 @@
     valid = valid_ref[0]
     own_ok = (own_row < 100) & (x * 100 + own_row < valid) & (count_ref[0] > 0)
     row_ok = jnp.where(own_ok, 1.0, 0.0).astype(F32)
-    hid_ref[0, 96:HALF] = jnp.zeros((HALF - 96, 384), F32)
-    hid_ref[0, 0:100] = img_ref[...]
-    img_copy = send(hid_ref.at[0, 0:HALF], hid_ref.at[0, HALF:ROWS], x_peer)
+    own_ref[...] = jnp.zeros((2, HALF, 384), F32)
+    own_ref[0, 0:100] = img_ref[...]
+    own_ref[1, 0:100] = ups_ref[...]
+    hid_ref[0, 0:HALF] = own_ref[0]
+    tok_ref[0, 0] = own_ref[0].astype(BF)
+    img_copy = send(tok_ref.at[0, 0], tok_ref.at[0, 1], x_peer)
 
     z_copies, y_copies, c_copies = {}, {}, {}
     for l in range(2):
@@ -424,15 +431,20 @@
             [jnp.where(first, mine, theirs), jnp.where(first, theirs, mine)], axis=0
         )
         w_ref[l, c, z, y] = chunk.astype(BF)
-        for a in (1, 0):
-            block = w_ref.at[l, c, z, y, :, PARTS[a]]
-            z_copies[l, a] = [send(block, block, at(z_next[d], y, c)) for d in (1, 2, 3)]
-            y_copies[l, a] = [send(block, block, y_peer)]
-
-    g_ref[96:HALF] = jnp.zeros((HALF - 96, 384), F32)
-    g_ref[0:100] = ups_ref[...]
-    g_ref[0:HALF] = g_ref[0:HALF] * row_ok
-    ups_copy = send(g_ref.at[0:HALF], g_ref.at[HALF:ROWS], x_peer)
+
+    def gather_z(l, a):
+        block = w_ref.at[l, c, z, y, :, PARTS[a]]
+        z_copies[l, a] = [send(block, block, at(z_next[d], y, c)) for d in (1, 2, 3)]
+        y_copies[l, a] = [send(block, block, y_peer)]
+
+    gather_z(0, 1)
+    gather_z(0, 0)
+
+    def ups_start():
+        own = own_ref[1] * row_ok
+        g_ref[0:HALF] = own
+        tok_ref[1, 0] = own.astype(BF)
+        return send(tok_ref.at[1, 0], tok_ref.at[1, 1], x_peer)
 
     def gather_y(l, a):
         for d in (1, 2, 3):
@@ -449,17 +461,21 @@
     def gather_end(l, a):
         c_copies[l, a].wait_recv()
 
+    def kept_rows(i):
+        return HALF if i in (3, 7) else ROWS
+
     def x_start(i, value):
         xs_ref[i] = value.astype(BF)
-        return [
-            send(xs_ref.at[i, HALF:ROWS], xr_ref.at[i, 0:HALF], x_peer),
-            send(xs_ref.at[i, 0:HALF], xr_ref.at[i, HALF:ROWS], x_peer),
-        ]
+        copies = [send(xs_ref.at[i, HALF:ROWS], xr_ref.at[i, 0:HALF], x_peer)]
+        if kept_rows(i) == ROWS:
+            copies.append(send(xs_ref.at[i, 0:HALF], xr_ref.at[i, HALF:ROWS], x_peer))
+        return copies
 
     def x_end(i, copies):
         for copy in copies:
             copy.wait_recv()
-        return xs_ref[i].astype(F32) + xr_ref[i].astype(F32)
+        kept = kept_rows(i)
+        return xs_ref[i, 0:kept].astype(F32) + xr_ref[i, 0:kept].astype(F32)
 
     def weight(l, half, start, size):
         return w_ref[l, half, :, :, :, pl.ds(start, size)].reshape(384, size)
@@ -511,25 +527,30 @@
         copies = x_start(2 * l + 1, dot(act_ref[l], weight(l, 1, 0, 768), 1, 1))
         yield
         branch = x_end(2 * l + 1, copies)
-        hid_ref[l + 1] = mid_ref[l] + (branch + vec(l, 5))
+        kept = kept_rows(2 * l + 1)
+        hid_ref[l + 1, 0:kept] = mid_ref[l, 0:kept] + (branch + vec(l, 5))
 
     gather_y(0, 1)
+    gather_z(1, 1)
+    img_copy.wait_recv()
+    hid_ref[0, HALF:ROWS] = tok_ref[0, 1].astype(F32)
+    ups_copy = ups_start()
+    step = attention(0)
+    next(step)
     gather_y(0, 0)
-    img_copy.wait_recv()
-    step = attention(0)
-    next(step)
     gather_core(0, 1)
+    gather_z(1, 0)
     gather_end(0, 1)
     next(step)
+    gather_y(1, 1)
     gather_core(0, 0)
-    gather_y(1, 1)
     next(step, None)
     step = feed(0)
     next(step)
     gather_end(0, 0)
     next(step)
+    gather_y(1, 0)
     gather_core(1, 1)
-    gather_y(1, 0)
     next(step, None)
     step = attention(1)
     next(step)
@@ -543,7 +564,8 @@
     next(step)
     next(step, None)
     out_ref[...] = (hid_ref[2, 0:HALF] * row_ok)[0:100]
-    ups_copy.wait()
+    ups_copy.wait_recv()
+    g_ref[HALF:ROWS] = tok_ref[1, 1].astype(F32)
 
     unit = {}
 
@@ -639,60 +661,118 @@
         keep(l, 1, 1024, dot(n1, gv, 0, 0))
         reduce_core(l, 1)
         yield
-        sm_ref[0, 8 * l + 1 : 8 * l + 2, 0:256] = col_sum(gq.astype(F32))
-        sm_ref[0, 8 * l + 1 : 8 * l + 2, 256:512] = col_sum(gv.astype(F32))
-        sm_ref[0, 8 * l + 2 : 8 * l + 3, 0:384] = col_sum(gm.astype(F32))
-        xhat, r = row_stats(hid_ref[l])
+        first_sums = [col_sum(v.astype(F32)) for v in (gq, gv, gm)]
+        kept = kept_rows(7 - 2 * l)
+        xhat, r = row_stats(hid_ref[l, 0:kept])
         e = x_end(7 - 2 * l, copies)
-        sm_ref[0, 8 * l + 2 : 8 * l + 3, 384:768] = col_sum(e * xhat)
-        sm_ref[0, 8 * l + 3 : 8 * l + 4, 0:384] = col_sum(e)
-        g_ref[...] = g + norm_grad(e, xhat, r, vec(l, 1))
+        sums = first_sums + [col_sum(e * xhat), col_sum(e)]
+        if l == 0:
+            at_row = 0
+            for total in sums:
+                for i in range(total.shape[1] // 128):
+                    late_ref[f_zx, at_row : at_row + 1] = total[:, 128 * i : 128 * i + 128]
+                    at_row += 1
+        else:
+            sm_ref[0, 9:10, 0:256] = sums[0]
+            sm_ref[0, 9:10, 256:512] = sums[1]
+            sm_ref[0, 10:11, 0:384] = sums[2]
+            sm_ref[0, 10:11, 384:768] = sums[3]
+            sm_ref[0, 11:12, 0:384] = sums[4]
+        g_ref[0:kept] = g[0:kept] + norm_grad(e, xhat, r, vec(l, 1))
 
     sm_ref[0] = jnp.zeros((16, 768), F32)
+    f_zx = z * 2 + x
+    f_yc = y * 2 + c
+    late_ref[f_zx] = jnp.zeros((24, 128), F32)
     step = feed_back(1)
     next(step)
     next(step, None)
+    reduce_y(1, 0)
     step = attention_back(1)
     next(step)
-    reduce_y(1, 0)
     next(step, None)
+    reduce_y(1, 1)
+    reduce_z(1, 0)
     step = feed_back(0)
     next(step)
-    reduce_z(1, 0)
-    reduce_y(1, 1)
     next(step, None)
-    step = attention_back(0)
-    next(step)
     reduce_y(0, 0)
     reduce_z(1, 1)
-    reduce_last(1, 0)
-    next(step, None)
-
     small = send(sm_ref.at[0], smr_ref.at[0], core_peer)
-    reduce_y(0, 1)
-    gimg_ref[...] = g_ref[0:HALF][0:100]
+    step = attention_back(0)
+    next(step)
     small.wait_recv()
     sm_ref[1] = sm_ref[0] + smr_ref[0]
     small = send(sm_ref.at[1], smr_ref.at[1], y_peer)
     reduce_z(0, 0)
-    reduce_last(1, 1)
+    reduce_y(0, 1)
     small.wait_recv()
     smz_ref[z] = sm_ref[1] + smr_ref[1]
     smalls = [send(smz_ref.at[z], smz_ref.at[z], at(z_next[d], y, c)) for d in (1, 2, 3)]
+    next(step, None)
+    lates = [send(late_ref.at[f_zx], late_ref.at[f_zx], peer) for peer in over_zx]
+    reduce_last(1, 0)
+    reduce_last(1, 1)
     reduce_z(0, 1)
-    reduce_last(0, 0)
     for small in smalls:
         small.wait_recv()
     small_ref[x] = ((smz_ref[0] + smz_ref[1]) + smz_ref[2]) + smz_ref[3]
     small = send(small_ref.at[x], small_ref.at[x], x_peer)
+    for late in lates:
+        late.wait_recv()
+    for t in range(2):
+        total = late_ref[t]
+        for zz in range(1, 4):
+            total = total + late_ref[2 * zz + t]
+        late_out_ref[f_yc, t] = total
+    lates = [send(late_out_ref.at[f_yc], late_out_ref.at[f_yc], peer) for peer in over_yc]
+    gimg_ref[...] = g_ref[0:HALF][0:100]
+    reduce_last(0, 0)
     reduce_last(0, 1)
+    for late in lates:
+        late.wait_recv()
+    late_sum_ref[...] = (late_out_ref[0] + late_out_ref[1]) + (late_out_ref[2] + late_out_ref[3])
     for copies in unit.values():
         for copy in copies:
             copy.wait_recv()
     small.wait_recv()
     for copy in started:
-        if copy is not ups_copy:
-            copy.wait_send()
+        copy.wait_send()
+
+
+def unpack_kernel(
+    output_in, gimg_in, gw_in, small_in, late_in,
+    output, gimg, qkv, qv, out_grad, out_bias, gain_one, shift_one, gain_two, shift_two,
+    up_grad, up_bias, down_grad, down_bias,
+):
+    output[...] = output_in[...]
+    gimg[...] = gimg_in[...]
+    for l in range(2):
+        up_grad[l] = gw_in[l, 0, :, 0:768]
+        down_grad[l] = gw_in[l, 1, :, 0:768].T
+        out_grad[l] = gw_in[l, 0, :, 768:1024].T[0:192]
+        qkv[l, 0] = gw_in[l, 0, :, 1024:1216]
+        qkv[l, 1] = gw_in[l, 1, :, 768:960]
+        qkv[l, 2] = gw_in[l, 1, :, 1024:1216]
+        row = 8 * l
+        for t in range(2):
+            up_bias[l : l + 1, 768 * t : 768 * t + 768] = small_in[t, row : row + 1, :]
+        gain_two[l : l + 1] = small_in[0, row + 3 : row + 4, 384:768]
+        shift_two[l : l + 1] = small_in[0, row + 4 : row + 5, 0:384]
+        down_bias[l : l + 1] = small_in[0, row + 4 : row + 5, 384:768]
+    for t in range(2):
+        for i in range(2):
+            qv[0, i : i + 1, 192 * t : 192 * t + 128] = late_in[t, 2 * i : 2 * i + 1, :]
+            qv[0, i : i + 1, 192 * t + 128 : 192 * t + 192] = late_in[t, 2 * i + 1 : 2 * i + 2, 0:64]
+            qv[1, i : i + 1, 192 * t : 192 * t + 192] = small_in[t, 9:10, 256 * i : 256 * i + 192]
+    for i in range(3):
+        lanes = slice(128 * i, 128 * i + 128)
+        out_bias[0:1, lanes] = late_in[0, 4 + i : 5 + i, :]
+        gain_one[0:1, lanes] = late_in[0, 7 + i : 8 + i, :] + late_in[1, 7 + i : 8 + i, :]
+        shift_one[0:1, lanes] = late_in[0, 10 + i : 11 + i, :] + late_in[1, 10 + i : 11 + i, :]
+    out_bias[1:2] = small_in[0, 10:11, 0:384]
+    gain_one[1:2] = small_in[0, 10:11, 384:768]
+    shift_one[1:2] = small_in[0, 11:12, 0:384]
 
 
 def fused_local(
@@ -722,17 +802,22 @@
     vmem = pl.BlockSpec(memory_space=pltpu.VMEM)
     smem = pl.BlockSpec(memory_space=pltpu.SMEM)
     V = pltpu.VMEM
-    output, grad_images, grads, small = pl.pallas_call(
+    output, grad_images, grads, small, late = pl.pallas_call(
         fused_kernel,
         out_shape=(
             jax.ShapeDtypeStruct((100, 384), F32),
             jax.ShapeDtypeStruct((100, 384), F32),
             jax.ShapeDtypeStruct((2, 2, 24, WIDE), F32),
             jax.ShapeDtypeStruct((2, 16, 768), F32),
+            jax.ShapeDtypeStruct((2, 24, 128), F32),
         ),
         in_specs=[smem] * 2 + [vmem] * 6,
-        out_specs=(vmem,) * 4,
+        out_specs=(vmem,) * 5,
         scratch_shapes=[
+            V((8, 24, 128), F32),
+            V((4, 2, 24, 128), F32),
+            V((2, HALF, 384), F32),
+            V((2, 2, HALF, 384), BF),
             V((2, 2, 4, 2, 48, WIDE), BF),
             V((2, 32, WIDE), BF),
             V((3, ROWS, 384), F32),
@@ -769,21 +854,19 @@
             flops=3 * 10**9, bytes_accessed=2 * 10**7, transcendentals=10**6
         ),
     )(image_count, valid_tokens, images[0], upstream[0], pack, vecs, qvb, upb)
-    up_grad = grads[:, 0, :, 0:768]
-    out_grad = turn(grads[:, 0, :, 768:960])
-    down_grad = turn(grads[:, 1, :, 0:768])
-    qkv_grad = jnp.stack(
-        [grads[:, 0, :, 1024:1216], grads[:, 1, :, 768:960], grads[:, 1, :, 1024:1216]], axis=1
-    )
-    small = small.reshape(2, 2, 8, 768)
-    up_bias_grad = jnp.concatenate([small[0, :, 0], small[1, :, 0]], axis=-1)
-    qv = small[:, :, 1, 0:512].reshape(2, 2, 2, 256)[..., 0:192]
-    qv_bias_grad = jnp.concatenate([qv[0], qv[1]], axis=-1)
-    row = lambda i, side: small[0, :, i, 384 * side : 384 * side + 384]
-    return (
-        output[None], grad_images[None], qkv_grad, qv_bias_grad, out_grad, row(2, 0),
-        row(2, 1), row(3, 0), row(3, 1), row(4, 0), up_grad, up_bias_grad, down_grad, row(4, 1),
-    )
+    shapes = [
+        (100, 384), (100, 384), (2, 3, 24, 192), (2, 2, 384), (2, 192, 24), (2, 384), (2, 384),
+        (2, 384), (2, 384), (2, 384), (2, 24, 768), (2, 1536), (2, 768, 24), (2, 384),
+    ]
+    results = pl.pallas_call(
+        unpack_kernel,
+        out_shape=[jax.ShapeDtypeStruct(shape, F32) for shape in shapes],
+        in_specs=[vmem] * 5,
+        out_specs=[vmem] * 14,
+        compiler_params=pltpu.CompilerParams(vmem_limit_bytes=16 * 2**20),
+    )(output, grad_images, grads, small, late)
+    return (results[0][None], results[1][None], *results[2:])
+
 
 def solution(mesh):
     in_specs = (

time: 107 us -> 99.6 us (0.931); the launches traced: 107 us -> 97.6 us
  Pallas kernels: 93.7 us -> 89.9 us
  local copies, waits for them, and re-layouts: 8.68 us -> 5.37 us
  other arithmetic: 2 us -> 0.05 us
    pallas_call x1, Pallas kernels: 93.7 us -> 88.9 us  [fused_local(): pl.pallas_call(fused_kernel, out_shape=(jax.ShapeDtypeStruct((100, 384),...]
    unnamed x39 -> x33, local copies, waits for them, and re-layouts: 7.04 us -> 5.18 us
    transpose x2 -> x0, local copies, waits for them, and re-layouts: 1.36 us -> none  [fused_local(): turn = lambda a: jnp.swapaxes(a, 1, 2)]
    concatenate x2 -> x0, other arithmetic: 1.27 us -> none  [the longest x1 0.67 us: fused_local(): qv_bias_grad = jnp.concatenate([qv[0], qv[1]], axis=-1)]
where the time goes in v2:
time: 99.6 us; the launch traced here: 97.6 us
  Pallas kernels  89.9 us (90%)
  local copies, waits for them, and re-layouts  5.37 us (5%)
  between operations  2.26 us (2%)
    pallas_call x1, Pallas kernels, fused_local(): pl.pallas_call(fused_kernel, out_shape=(jax.ShapeDtypeStruct((100, 384),...  88.9 us
    unnamed x33, local copies, waits for them, and re-layouts  5.18 us

profile of v2, /device:TPU:0, one launch (start us, length us, event | category | flops | bytes accessed | tf_op | source)
XLA Modules:
  0.0 97.6 jit_solution(14603769644658808491)
XLA Ops:
  0.6 0.0 copy-start
  0.7 0.0 copy-start.7
  0.7 0.0 copy-start.8
  0.7 0.0 copy-start.9
  0.7 0.0 copy-start.10
  0.7 0.0 copy-start.11
  0.7 0.0 copy-start.12
  0.7 0.0 copy-start.13
  0.7 0.0 copy-start.3
  2.1 0.0 copy-done.7
  2.1 0.0 copy-done.8
  2.1 0.0 copy-done.9
  2.1 0.0 copy-done.10
  2.2 0.0 copy-done.11
  2.2 0.0 copy-done.12
  2.2 0.0 copy-done.13
  2.2 0.1 constant_dynamic-slice_fusion.1
  2.3 0.0 copy-done
  2.3 0.0 copy-start.6
  2.4 0.1 stack.41.vec_ref
  2.4 0.0 copy-done.3
  2.4 0.0 copy-start.4
  2.4 0.0 copy-start.5
  2.5 0.6 copy-done.6
  3.1 0.2 copy-done.4
  3.3 0.0 copy-done.5
  3.4 0.0 copy-start.1
  3.4 0.0 copy-start.2
  3.4 0.9 copy-done.1
  4.3 0.1 copy-done.2
  4.4 88.9 %shard_map.263 = (f32[100,384]{1,0:T(8,128)S(1)}, f32[100,384]{1,0:T(8,128)S(1)}, f32[2,2,24,1280]{3,2,1,0:T(8,128)S(1)}, f32[2,16,768]{2,1,0:T(8,128)S(1)}, f32[2,24,128]{2,1,0:T(8,128)S(1)}) custom-call(s32[1]{0:T(128)S(6)} %copy.44.count_ref, s32[1]{0:T(128)S(6)} %copy.45.valid_ref, f32[100,384]{1,0:T(8,128)S(1)} %get-tuple-element.72.img_ref, ...), custom_call_target="tpu_custom_call" | custom-call | flops 3000000000 | bytes 20000000 | tf_op jit(solution)/shard_map/pallas_call | solution.py:805
  93.3 1.0 %shard_map.264 = (f32[100,384]{1,0:T(8,128)S(1)}, f32[100,384]{1,0:T(8,128)S(1)}, f32[2,3,24,192]{3,2,1,0:T(8,128)}, f32[2,2,384]{2,1,0:T(2,128)}, f32[2,192,24]...) custom-call(f32[100,384]{1,0:T(8,128)S(1)} %get-tuple-element.33.out, ...), custom_call_target="tpu_custom_call" | custom-call | tf_op jit(solution)/shard_map/pallas_call | solution.py:861
  94.3 0.8 copy.33
  95.1 0.8 copy.34
  96.0 0.7 copy.35
  96.7 0.9 copy.36
  (13 shorter events, 0.1 us)
Async XLA Ops:
  0.6 1.7 %copy-start = (f32[2,1536]{1,0:T(2,128)S(1)}, f32[2,1536]{1,0:T(2,128)}, u32[]{:S(2)}) copy-start(f32[2,1536]{1,0:T(2,128)} %param.29) | copy-start | bytes 36868
  0.7 1.4 %copy-start.7 = (f32[2,384]{1,0:T(2,128)S(1)}, f32[2,384]{1,0:T(2,128)}, u32[]{:S(2)}) copy-start(f32[2,384]{1,0:T(2,128)} %param.23) | copy-start | bytes 9220
  0.7 1.4 %copy-start.8 = (f32[2,384]{1,0:T(2,128)S(1)}, f32[2,384]{1,0:T(2,128)}, u32[]{:S(2)}) copy-start(f32[2,384]{1,0:T(2,128)} %param.24) | copy-start | bytes 9220
  0.7 1.4 %copy-start.9 = (f32[2,384]{1,0:T(2,128)S(1)}, f32[2,384]{1,0:T(2,128)}, u32[]{:S(2)}) copy-start(f32[2,384]{1,0:T(2,128)} %param.25) | copy-start | bytes 9220
  0.7 1.4 %copy-start.10 = (f32[2,384]{1,0:T(2,128)S(1)}, f32[2,384]{1,0:T(2,128)}, u32[]{:S(2)}) copy-start(f32[2,384]{1,0:T(2,128)} %param.26) | copy-start | bytes 9220
  0.7 1.5 %copy-start.11 = (f32[2,384]{1,0:T(2,128)S(1)}, f32[2,384]{1,0:T(2,128)}, u32[]{:S(2)}) copy-start(f32[2,384]{1,0:T(2,128)} %param.27) | copy-start | bytes 9220
  0.7 1.5 %copy-start.12 = (f32[2,384]{1,0:T(2,128)S(1)}, f32[2,384]{1,0:T(2,128)}, u32[]{:S(2)}) copy-start(f32[2,384]{1,0:T(2,128)} %param.31) | copy-start | bytes 9220
  0.7 1.5 %copy-start.13 = (f32[2,2,384]{2,1,0:T(2,128)S(1)}, f32[2,2,384]{2,1,0:T(2,128)}, u32[]{:S(2)}) copy-start(f32[2,2,384]{2,1,0:T(2,128)} %param.21) | copy-start | bytes 18436
  0.7 1.7 %copy-start.3 = (bf16[2,3,24,192]{3,2,1,0:T(8,128)(2,1)S(1)}, bf16[2,3,24,192]{3,2,1,0:T(8,128)(2,1)}, u32[]{:S(2)}) copy-start(bf16[2,3,24,192]{3,2,1,0:T(8,128)(2,1)} %param.20) | copy-start | bytes 165892
  2.3 0.7 copy-start.6
  2.4 0.9 copy-start.4
  2.4 0.9 copy-start.5
  3.4 0.9 copy-start.1
  3.4 1.0 %copy-start.2 = (f32[1,100,384]{2,0,1:T(1,128)S(1)}, f32[1,100,384]{2,0,1:T(1,128)}, u32[]{:S(2)}) copy-start(f32[1,100,384]{2,0,1:T(1,128)} %param.16) | copy-start | bytes 460804
